TPU v7x, 32 devices: a whole 2x2x4 slice. The times are simulated.
32 devices in a mesh: scan: 16 (over z, y, x), mode: 2 (over core).
Axes of the slice: x: 2, y: 2, z: 4, core: 2. Of those that a mesh axis runs over, the one named last changes fastest.
Arguments:
- object_field: float32 [2, 640, 1152], P(None, 'scan'), may hold values from -4.5 to 4.5
- probe: float32 [8, 2, 512, 512], P('mode'), may hold values from -1.5 to 1.5
- amplitude: float32 [16, 512, 512], P('scan'), may hold values from 0.2 to 1.8
- pos_row: int32 [16], P('scan'), may hold values from 0 to 128, as said below
- pos_col: int32 [16], P('scan'), may hold values from 0 to 640, as said below
- strip_of: int32 [16], P('scan'), may hold values from 0 to 15, each once
Outputs:
- object_grad: float32 [2, 640, 1152], P(None, 'scan')
- probe_grad: float32 [8, 2, 512, 512], P('mode')
Inputs may be any that keep to these rules, and one draw needn't show every extreme that they name: Pattern p covers object rows pos_row[p] to pos_row[p] + 511; the smallest and the largest allowed value both occur. Pattern p covers object columns pos_col[p] to pos_col[p] + 511; the smallest and the largest allowed value both occur.
All inputs are finite; a program needn't handle non-finite values.
Results may differ from a plain program's by a relative error of at most 0.0055.
The roundings to bfloat16 on the way count: a program that leaves them out, or rounds other values in their place, can miss the bound.
Values may be sent and summed in bfloat16 or wider, within the bound.
A program may use at most 128 MiB of HBM per device.

v0:
```python
import math

import jax
import jax.numpy as jnp
from jax import lax
from jax.sharding import PartitionSpec as P


def dft_table(sign_factor, probe_size):
    positions = jnp.arange(probe_size, dtype=jnp.int32)
    products = positions[:, None] * positions[None, :] % probe_size
    angle_table = products.astype(jnp.float32) * (2.0 * math.pi / probe_size)
    norm_scale = 1.0 / math.sqrt(probe_size)
    cosine = jnp.cos(angle_table) * norm_scale
    sine_part = jnp.sin(angle_table) * (sign_factor * norm_scale)
    return jnp.stack([jnp.stack([cosine, sine_part]), jnp.stack([-sine_part, cosine])]).astype(
        jnp.bfloat16
    )


def transform(field_wave, matrix_table):
    half_wave = jnp.einsum(
        "oiab,pmibx->pmoax", matrix_table, field_wave, preferred_element_type=jnp.float32
    ).astype(jnp.bfloat16)
    return jnp.einsum(
        "pmiax,oixy->pmoay", half_wave, matrix_table, preferred_element_type=jnp.float32
    )


def shards(object_field, probe, amplitude, pos_row, pos_col, strip_of):
    probe_size = probe.shape[-1]
    strip_rows = object_field.shape[1]
    obj_cols = object_field.shape[2]
    pat_count = pos_row.shape[0]
    devices = lax.axis_size("scan")
    held_rows = devices * strip_rows
    all_strips, all_cols = (
        lax.all_gather(strip_of, "scan", axis=0, tiled=True),
        lax.all_gather(pos_col, "scan", axis=0, tiled=True),
    )
    device_ids = jnp.arange(devices, dtype=jnp.int32)
    owner_of = jnp.sum(
        jnp.where(all_strips[None, :] == device_ids[:, None], device_ids[None, :], 0), axis=1
    )
    inside_rows = jnp.tile(jnp.arange(strip_rows, dtype=jnp.int32), devices)
    held_of_window = jnp.repeat(owner_of, strip_rows) * strip_rows + inside_rows
    window_of_held = jnp.repeat(all_strips, strip_rows) * strip_rows + inside_rows

    def patch_rows(row_start):
        return lax.dynamic_slice_in_dim(held_of_window, row_start, probe_size)

    held_index = jax.vmap(patch_rows)(pos_row)
    object_half = object_field.astype(jnp.bfloat16)
    gathered = lax.all_gather(object_half, "scan", axis=1, tiled=True)

    def take_patch(rows_wanted, col_start):
        band_rows = jnp.take(gathered, rows_wanted, axis=1)
        return lax.dynamic_slice_in_dim(band_rows, col_start, probe_size, 2)

    patches = jax.vmap(take_patch)(held_index, pos_col)
    patch_wide = patches.astype(jnp.float32)
    patch_re = patch_wide[:, None, 0]
    patch_im = patch_wide[:, None, 1]
    probe_re = probe[:, 0]
    probe_im = probe[:, 1]
    exit_re = probe_re * patch_re - probe_im * patch_im
    exit_im = probe_re * patch_im + probe_im * patch_re
    exit_wave = jnp.stack([exit_re, exit_im], axis=2).astype(jnp.bfloat16)
    forward = dft_table(1.0, probe_size)
    inverse = dft_table(-1.0, probe_size)
    far_field = transform(exit_wave, forward)
    local_power = jnp.sum(
        far_field[:, :, 0] * far_field[:, :, 0] + far_field[:, :, 1] * far_field[:, :, 1], axis=1
    )
    intensity = lax.psum(local_power, "mode")
    scale_factor = 1.0 - amplitude / jnp.sqrt(jnp.maximum(intensity, 0.25))
    residual_wave = (far_field * scale_factor[:, None, None]).astype(jnp.bfloat16)
    back_wave = transform(residual_wave, inverse)
    back_re = back_wave[:, :, 0]
    back_im = back_wave[:, :, 1]
    grad_re = jnp.sum(probe_re * back_re + probe_im * back_im, axis=1)
    grad_im = jnp.sum(probe_re * back_im - probe_im * back_re, axis=1)
    patch_grad = jnp.stack([grad_re, grad_im], axis=1)
    term_re = jnp.sum(patch_re * back_re + patch_im * back_im, axis=0)
    term_im = jnp.sum(patch_re * back_im - patch_im * back_re, axis=0)
    probe_grad = lax.psum(jnp.stack([term_re, term_im], axis=1), "scan")
    patch_grad = lax.psum(patch_grad, "mode")

    def band_of(grad_piece, row_start):
        band_rows = jnp.zeros((2, held_rows, probe_size), jnp.float32)
        band_rows = lax.dynamic_update_slice_in_dim(band_rows, grad_piece, row_start, 1)
        return jnp.take(band_rows, window_of_held, axis=1)

    bands = jax.vmap(band_of)(patch_grad, pos_row)
    received = lax.all_to_all(bands, "scan", split_axis=2, concat_axis=0, tiled=True)

    def add_piece(slot_index, strip_total):
        col_start = all_cols[slot_index]
        current = lax.dynamic_slice_in_dim(strip_total, col_start, probe_size, 2)
        return lax.dynamic_update_slice_in_dim(
            strip_total, current + received[slot_index], col_start, 2
        )

    object_grad = lax.fori_loop(
        0, devices * pat_count, add_piece, jnp.zeros((2, strip_rows, obj_cols), jnp.float32)
    )
    return (object_grad, probe_grad)


def solution(mesh):
    return jax.shard_map(
        shards,
        mesh=mesh,
        in_specs=(
            P(None, "scan", None),
            P("mode", None, None, None),
            P("scan", None, None),
            P("scan"),
            P("scan"),
            P("scan"),
        ),
        out_specs=(P(None, "scan", None), P("mode", None, None, None)),
        check_vma=False,
    )
```

profile of v0, /device:TPU:0, one launch (start us, length us, event | category | flops | bytes accessed | tf_op | source)
XLA Modules:
  0.0 562.3 jit_solution(8527928719411964411)
XLA Ops:
  11.1 7.8 %fusion.57 = (f32[4,1,512,512]{3,2,1,0:T(8,128)}, f32[4,1,512,512]{3,2,1,0:T(8,128)}) fusion(f32[4,2,512,512]{3,2,1,0:T(8,128)} %param.11), kind=kLoop, calls=%fused_computation.103 | loop fusion | bytes 16777216 | tf_op jit(solution)/shard_map/slice | solution.py:64
  18.9 5.3 copy.123
  24.1 5.3 copy.122
  31.5 16.2 %all-reduce.3 = (s32[16]{0:T(128)S(1)}, s32[16]{0:T(128)S(1)}) all-reduce(s32[16]{0:T(128)S(1)} %dynamic-update-slice.5, s32[16]{0:T(128)S(1)} %dynamic-update-slice.6), channel_id=1, replica_groups=mesh['scan'=16,'mode'=2] {'scan'}, use_global_device_ids=true, to_apply=%add.1 | all-reduce | flops 32 | bytes 256
  48.1 4.0 multiply_convert_fusion.3
  52.1 4.4 multiply_convert_fusion.1
  56.5 4.0 negate_convert_fusion
  62.7 17.7 %all-gather.2.cloned.1.call-done = bf16[2,640,1152]{2,0,1:T(2,128)(2,1)} async-done(((bf16[2,40,1152]{2,0,1:T(2,128)(2,1)}), bf16[2,640,1152]{2,0,1:T(2,128)(2,1)}) %all-gather.2.cloned.1.call-update) | async-done | bytes 2949136 | tf_op jit(solution)/shard_map/all_gather | solution.py:54
  80.4 28.9 %gather_fusion = bf16[512,2,1152]{2,1,0:T(2,128)(2,1)S(1)} fusion(bf16[2,640,1152]{2,0,1:T(2,128)(2,1)} %all-gather.2.cloned.1.call-done, s32[1024]{0:T(1024)S(1)} %pad_clamp_fusion.1), kind=kCustom, calls=%fused_computation | custom fusion | bytes 4720640 | tf_op jit(solution)/shard_map/vmap(jit(_take))/gather | solution.py:57
  109.2 3.7 fusion.40
  117.4 6.4 %fusion.23 = bf16[4,1,512,512]{2,3,1,0:T(8,128)(2,1)} fusion(f32[4,1,512,512]{2,3,0,1:T(8,128)} %copy.123, f32[4,1,512,512]{2,3,0,1:T(8,128)} %copy.122, f32[512,512]{0,1:T(8,128)S(1)} %bitcast.213, f32[512,512]{0,1:T(8,128)S(1)} %bitcast.216), kind=kLoop, calls=%fused_computation.42 | loop fusion | flops 4194304 | bytes 12582912 | tf_op jit(solution)/shard_map/convert.1
  123.8 2.8 fusion.31
  126.6 15.1 %fusion.27 = f32[1,4,2,512,512]{3,4,1,2,0:T(8,128)} fusion(bf16[1,2,512,512]{3,2,1,0:T(8,128)(2,1)S(1)} %copy-done.3, bf16[1,2,512,512]{3,2,1,0:T(8,128)(2,1)} %get-tuple-element.158, bf16[4,1,512,512]{2,3,1,0:T(8,128)(2,1)} %fusion.23, bf16[4,1,512,512]{2,3,1,0:T(8,128)(2,1)} %fusion.31), kind=kOutput, calls=%fused_computation.44 | convolution fusion | flops 8608808960 | bytes 14680064 | tf_op jit(solution)/shard_map/pmiax,oixy->pmoay/dot_general | solution.py:25
  141.8 5.9 %fusion.12 = f32[512,512]{0,1:T(8,128)} fusion(f32[1,4,2,512,512]{3,4,1,2,0:T(8,128)} %fusion.27), kind=kLoop, calls=%fused_computation.20 | loop fusion | flops 3932160 | bytes 9437184 | tf_op jit(solution)/shard_map/reduce_sum | solution.py:72
  149.3 17.2 %all-reduce.8.cloned.1.call-done = f32[1,512,512]{1,2,0:T(8,128)} async-done(((f32[1,512,512]{1,2,0:T(8,128)}), f32[1,512,512]{1,2,0:T(8,128)}) %all-reduce.8.cloned.1.call-update) | async-done | bytes 1048592 | tf_op jit(solution)/shard_map/psum | solution.py:75
  166.5 2.5 subtract_bitcast_fusion
  169.0 15.9 %fusion.24 = f32[1,4,2,512,512]{3,4,1,2,0:T(8,128)} fusion(bf16[1,2,512,512]{3,2,1,0:T(8,128)(2,1)} %get-tuple-element.159, bf16[1,2,512,512]{3,2,1,0:T(8,128)(2,1)} %get-tuple-element.156, f32[1,4,2,512,512]{3,4,1,2,0:T(8,128)} %fusion.27, f32[512,512]{0,1:T(8,128)} %subtract_bitcast_fusion), kind=kOutput, calls=%fused_computation.43 | convolution fusion | flops 8602517504 | bytes 19922944 | tf_op jit(solution)/shard_map/pmiax,oixy->pmoay/dot_general | solution.py:25
  184.9 8.1 %fusion.17 = (f32[512,512]{0,1:T(8,128)S(1)}, f32[512,512]{0,1:T(8,128)}) fusion(f32[4,1,512,512]{2,3,0,1:T(8,128)} %copy.123, f32[4,1,512,512]{2,3,0,1:T(8,128)} %copy.122, f32[1,4,2,512,512]{3,4,1,2,0:T(8,128)} %fusion.24), kind=kLoop, calls=%fused_computation.33 | loop fusion | flops 7864320 | bytes 18874368 | tf_op jit(solution)/shard_map/reduce_sum | solution.py:81
  193.0 3.6 copy.120
  198.5 4.8 pad_maximum_fusion.3
  203.7 4.8 fusion.3
  208.5 4.7 pad_maximum_fusion
  214.6 2.7 and_reduce_fusion
  217.3 8.6 %all-reduce.10.cloned.1.call-done = f32[1,2,512,512]{3,1,2,0:T(2,128)} async-done(((f32[1,2,512,512]{3,1,2,0:T(2,128)}), f32[1,2,512,512]{3,1,2,0:T(2,128)}) %all-reduce.10.cloned.1.call-update) | async-done | bytes 2097168 | tf_op jit(solution)/shard_map/psum | solution.py:87
  226.6 3.9 bitcast_dynamic-update-slice_fusion
  230.5 5.5 gather_fusion.1
  236.1 5.3 fusion.30
  241.4 6.8 %all-to-all-start = ((f32[1,2,640,512]{3,1,0,2:T(2,128)}), f32[1,2,640,512]{3,1,0,2:T(2,128)S(1)}, u32[]{:S(2)}, u32[]{:S(2)}) async-start(f32[1,2,640,512]{3,1,0,2:T(2,128)} %fusion.30), calls=%async_computation | async-start | bytes 5242880 | tf_op jit(solution)/shard_map/all_to_all | solution.py:95
  248.2 89.7 %all-to-all-done = f32[1,2,640,512]{3,1,0,2:T(2,128)S(1)} async-done(((f32[1,2,640,512]{3,1,0,2:T(2,128)}), f32[1,2,640,512]{3,1,0,2:T(2,128)S(1)}, u32[]{:S(2)}, u32[]{:S(2)}) %all-to-all-start) | async-done | bytes 2621472 | tf_op jit(solution)/shard_map/all_to_all | solution.py:95
  340.0 72.9 %while.16 = (s32[]{:T(128)}, f32[2,40,1152]{2,1,0:T(8,128)S(1)}, s32[16]{0:T(128)S(1)}, f32[16,2,40,512]{3,2,0,1:T(8,128)}, s32[]{:T(128)}, /*index=5*/s32[]{:T(128)}, s32[]{:T(128)}) while((s32[]{:T(128)}, f32[2,40,1152]{2,1,0:T(8,128)S(1)}, s32[16]{0:T(128)S(1)}, f32[16,2,40,512]{3,2,0,1:T(8,128)}, s32[]{:T(128)}, /*index=5*/s32[]{:T(128)}, ...), condition=%wide.region_8.9_spmd, body=%wide.region_7.8_spmd.sunk | while | flops 40965 | bytes 819343 | solution.py:104
  412.9 132.7 %all-reduce.12.cloned.1.call-done = f32[4,2,512,512]{2,3,1,0:T(8,128)} async-done(((f32[4,2,512,512]{2,3,1,0:T(8,128)}), f32[4,2,512,512]{2,3,1,0:T(8,128)}) %all-reduce.12.cloned.1.call-update) | async-done | bytes 8388624 | tf_op jit(solution)/shard_map/psum | solution.py:86
  545.6 9.9 %copy.98 = f32[4,2,512,512]{3,2,1,0:T(8,128)} copy(f32[4,2,512,512]{2,3,1,0:T(8,128)} %all-reduce.12.cloned.1.call-done) | data formatting | bytes 16777216
  (101 shorter events, 62.2 us)
Async XLA Ops:
  7.2 73.2 %all-gather.2.cloned.1.call-start = ((), (), s32[]{:S(2)}) async-start(), calls=%async_computation.1 | async-start | bytes 3133440 | tf_op jit(solution)/shard_map/all_gather | solution.py:54
  9.1 157.4 %all-reduce.8.cloned.1.call-start = ((), (), s32[]{:S(2)}) async-start(), calls=%async_computation.2 | async-start | bytes 2097152 | tf_op jit(solution)/shard_map/psum | solution.py:75
  24.1 5.3 copy-start.6
  117.4 6.4 %copy-start = (f32[4,1,512,512]{2,3,0,1:T(8,128)S(1)}, f32[4,1,512,512]{2,3,0,1:T(8,128)}, u32[]{:S(2)}) copy-start(f32[4,1,512,512]{2,3,0,1:T(8,128)} %copy.123) | copy-start | bytes 12582916
  117.4 6.4 %copy-start.1 = (f32[4,1,512,512]{2,3,0,1:T(8,128)S(1)}, f32[4,1,512,512]{2,3,0,1:T(8,128)}, u32[]{:S(2)}) copy-start(f32[4,1,512,512]{2,3,0,1:T(8,128)} %copy.122) | copy-start | bytes 12582916
  123.8 2.8 copy-start.3
  147.7 78.2 %all-reduce.10.cloned.1.call-start = ((), (), s32[]{:S(2)}) async-start(), calls=%async_computation.3 | async-start | bytes 4194304 | tf_op jit(solution)/shard_map/psum | solution.py:87
  203.4 342.3 %all-reduce.12.cloned.1.call-start = ((), (), s32[]{:S(2)}) async-start(), calls=%async_computation.4 | async-start | bytes 16777216 | tf_op jit(solution)/shard_map/psum | solution.py:86
  213.2 0.7 copy-start.5
  213.2 1.4 copy-start.4
  241.4 96.5 %all-to-all-start = ((f32[1,2,640,512]{3,1,0,2:T(2,128)}), f32[1,2,640,512]{3,1,0,2:T(2,128)S(1)}, u32[]{:S(2)}, u32[]{:S(2)}) async-start(f32[1,2,640,512]{3,1,0,2:T(2,128)} %fusion.30), calls=%async_computation | async-start | bytes 5242880 | tf_op jit(solution)/shard_map/all_to_all | solution.py:95
  412.9 142.6 %copy-start.2 = (f32[2,40,1152]{2,1,0:T(8,128)}, f32[2,40,1152]{2,1,0:T(8,128)S(1)}, u32[]{:S(2)}) copy-start(f32[2,40,1152]{2,1,0:T(8,128)S(1)} %get-tuple-element.134) | copy-start | bytes 1105924
Sparse Core Ops, SparseCore 0:
  11.4 68.9 all-gather.1
  147.8 18.6 all-reduce.7
  203.5 22.3 all-reduce.9
  232.3 313.2 all-reduce.11
where the time goes:
time: 569 us; the launch traced here: 562 us
  waiting for transfers between devices  266 us (47%)
  local copies, waits for them, and re-layouts  109 us (19%)
  other arithmetic  87.4 us (15%)
  matrix products  31 us (5%)
  loops' own time  29.7 us (5%)
  blocking collectives  16.2 us (3%)
  between operations  16.2 us (3%)
  starting transfers between devices  7.2 us (1%)
    psum x1, waiting for transfers between devices, shards(): probe_grad = lax.psum(jnp.stack([term_re, term_im], axis=1), 'scan')  133 us
    all_to_all x1, waiting for transfers between devices, shards(): lax.all_to_all(bands, 'scan', split_axis=2, concat_axis=0, tiled=True)  89.7 us
    dot_general x2, matrix products, transform(): jnp.einsum('pmiax,oixy->pmoay', half_wave, matrix_table, preferred_elemen...  31 us
    another operation x1, loops' own time, shards(): lax.fori_loop(0, devices * pat_count, add_piece, jnp.zeros((2, strip_rows...  29.7 us
    gather x1, local copies, waits for them, and re-layouts, take_patch(): band_rows = jnp.take(gathered, rows_wanted, axis=1)  28.9 us
    unnamed x24, local copies, waits for them, and re-layouts  26.3 us
    another operation x6, other arithmetic  24.3 us
    all_gather x1, waiting for transfers between devices, shards(): gathered = lax.all_gather(object_half, 'scan', axis=1, tiled=True)  17.7 us
  transfers between devices with their start and end apart: 5, of which 5 were waited for; matrix products, arithmetic and copies ran while one was open for 20% of the time, Pallas kernels for 0%

commit v1 on v0

v1 whole, which is shorter than its diff:
```python
import math

import jax
import jax.numpy as jnp
import numpy as np
from jax import lax
from jax.experimental import pallas as pl
from jax.experimental.pallas import tpu as pltpu
from jax.sharding import PartitionSpec as P

F32 = jnp.float32
BF16 = jnp.bfloat16
LANES = 128
META = 16
TILE = 256
PARAMS = pltpu.CompilerParams(vmem_limit_bytes=56 * 1024 * 1024)
VMEM = pl.BlockSpec(memory_space=pltpu.VMEM)
SMEM = pl.BlockSpec(memory_space=pltpu.SMEM)


def dft_tables(size):
    positions = np.arange(size, dtype=np.int32)
    angles = (positions[:, None] * positions[None, :] % size).astype(np.float32)
    angles = angles * np.float32(2.0 * math.pi / size)
    norm = np.float32(1.0 / math.sqrt(size))
    cosine, sine = np.cos(angles) * norm, np.sin(angles) * norm
    forward = np.block([[cosine, sine], [-sine, cosine]])
    inverse = np.block([[cosine, -sine], [sine, cosine]])
    return jnp.asarray(forward, BF16), jnp.asarray(inverse, BF16)


def cut_kernel(strips, row, col, held, patch, window):
    count, rows = held.shape[0], (held.shape[1] - META) // 2
    size, cols = patch.shape[-1], held.shape[-1]
    wide = size + LANES

    def place(j, carry):
        both = held[j][: 2 * rows].astype(F32)
        at = pl.ds(pl.multiple_of(strips[j] * rows, 8), rows)
        window[0, at, :cols] = both[:rows]
        window[1, at, :cols] = both[rows:]
        return carry

    lax.fori_loop(0, count, place, 0)
    across = pl.ds(pl.multiple_of(col[0] // LANES * LANES, LANES), wide)
    back = lax.rem(wide - lax.rem(col[0], LANES), wide)
    up = lax.rem(72 - lax.rem(row[0], 8), 72)
    for c in range(2):

        def cut(i, carry, c=c):
            block = window[c, pl.ds(pl.multiple_of(row[0] // 8 * 8 + i * 64, 8), 72), across]
            block = pltpu.roll(block, up, 0)[:64]
            patch[c, pl.ds(pl.multiple_of(i * 64, 64), 64), :] = pltpu.roll(block, back, 1)[:, :size]
            return carry

        lax.fori_loop(0, size // 64, cut, 0)


def forward_kernel(probe, patch, left, right, far, power, wave, half):
    size = patch.shape[-1]

    def leave(i, carry):
        at = pl.ds(pl.multiple_of(i * 64, 64), 64)
        low = pl.ds(pl.multiple_of(size + i * 64, 64), 64)
        pr, pi, xr, xi = probe[0, 0, at], probe[0, 1, at], patch[0, at], patch[1, at]
        wave[at] = (pr * xr - pi * xi).astype(BF16)
        wave[low] = (pr * xi + pi * xr).astype(BF16)
        return carry

    lax.fori_loop(0, size // 64, leave, 0)
    rows_product(left, wave, half)
    first = pl.program_id(0) == 0

    def across(i, carry):
        at = pl.ds(pl.multiple_of(i * TILE, TILE), TILE)
        both = jnp.dot(half[at], right[...], preferred_element_type=F32)
        re, im = both[:, :size], both[:, size:]
        far[0, 0, at] = re
        far[0, 1, at] = im
        here = re * re + im * im
        power[at] = jnp.where(first, here, power[at] + here)
        return carry

    lax.fori_loop(0, size // TILE, across, 0)


def rows_product(left, wave, half):
    size = wave.shape[-1]
    for c in range(2):

        def down(i, carry, c=c):
            at = pl.ds(pl.multiple_of(c * size + i * TILE, TILE), TILE)
            to = pl.ds(pl.multiple_of(i * TILE, TILE), TILE)
            product = jnp.dot(left[at], wave[...], preferred_element_type=F32)
            half[to, c * size : (c + 1) * size] = product.astype(BF16)
            return carry

        lax.fori_loop(0, size // TILE, down, 0)


def backward_kernel(far, probe, patch, measured, power, left, right, term, grad, scale, wave, half):
    size = patch.shape[-1]
    first = pl.program_id(0) == 0

    @pl.when(first)
    def _():
        total = jnp.maximum(power[...], 0.25)
        scale[...] = 1.0 - measured[...] / jnp.sqrt(total)

    def residual(i, carry):
        at = pl.ds(pl.multiple_of(i * 64, 64), 64)
        low = pl.ds(pl.multiple_of(size + i * 64, 64), 64)
        wave[at] = (far[0, 0, at] * scale[at]).astype(BF16)
        wave[low] = (far[0, 1, at] * scale[at]).astype(BF16)
        return carry

    lax.fori_loop(0, size // 64, residual, 0)
    rows_product(left, wave, half)

    def across(i, carry):
        at = pl.ds(pl.multiple_of(i * TILE, TILE), TILE)
        both = jnp.dot(half[at], right[...], preferred_element_type=F32)
        br, bi = both[:, :size], both[:, size:]
        pr, pi, xr, xi = probe[0, 0, at], probe[0, 1, at], patch[0, at], patch[1, at]
        term[0, 0, at] = (xr * br + xi * bi).astype(BF16)
        term[0, 1, at] = (xr * bi - xi * br).astype(BF16)
        re, im = pr * br + pi * bi, pr * bi - pi * br
        grad[0, at] = jnp.where(first, re, grad[0, at] + re)
        grad[1, at] = jnp.where(first, im, grad[1, at] + im)
        return carry

    lax.fori_loop(0, size // TILE, across, 0)


def place_kernel(strips, row, grad, out, padded):
    count, parts, rows, size = out.shape
    padded[...] = jnp.zeros_like(padded)
    padded[:, rows : rows + size, :] = grad[...]

    def one(j, carry):
        start = jnp.clip(strips[j] * rows - row[0], -rows, size) + rows
        base = pl.ds(pl.multiple_of(start // 8 * 8, 8), rows + 8)
        up = lax.rem(rows + 8 - lax.rem(start, 8), rows + 8)
        for k in range(parts):
            out[j, k] = pltpu.roll(padded[k, base, :], up, 0)[:rows]
        return carry

    lax.fori_loop(0, count, one, 0)


def add_kernel(cols, received, out, total):
    count, parts, rows, size = received.shape
    total[...] = jnp.zeros_like(total)
    edge = jnp.zeros((rows, LANES), F32)

    def one(j, carry):
        across = pl.ds(pl.multiple_of(cols[j] // LANES * LANES, LANES), size + LANES)
        shift = lax.rem(cols[j], LANES)
        for k in range(parts):
            piece = jnp.concatenate([received[j, k], edge], axis=1)
            total[k, :, across] += pltpu.roll(piece, shift, 1)
        return carry

    lax.fori_loop(0, count, one, 0)
    out[...] = total[:, :, : out.shape[-1]]


def shards(object_field, probe, amplitude, pos_row, pos_col, strip_of):
    size = probe.shape[-1]
    modes = probe.shape[0]
    rows, cols = object_field.shape[1], object_field.shape[2]
    devices, groups = lax.axis_size("scan"), lax.axis_size("mode")
    padded_cols = cols + LANES
    forward, inverse = dft_tables(size)

    def swap(x):
        return lax.ppermute(x, "mode", [(0, 1), (1, 0)])

    lane = lax.broadcasted_iota(jnp.int32, (META, cols), 1)
    numbers = jnp.where(lane == 0, strip_of[0], jnp.where(lane == 1, pos_col[0] // LANES, pos_col[0] % LANES))
    packed = jnp.concatenate([object_field.reshape(2 * rows, cols).astype(BF16), numbers.astype(BF16)])
    held = lax.all_gather(packed, "scan", axis=0)
    numbers = held[:, 2 * rows, :3].astype(jnp.int32)
    strips = numbers[:, 0]
    all_cols = numbers[:, 1] * LANES + numbers[:, 2]

    wave_shape = jax.ShapeDtypeStruct((2, size, size), F32)
    patch = pl.pallas_call(
        cut_kernel,
        out_shape=wave_shape,
        in_specs=[SMEM, SMEM, SMEM, VMEM],
        out_specs=VMEM,
        scratch_shapes=[pltpu.VMEM((2, devices * rows + 8, padded_cols), F32)],
        compiler_params=PARAMS,
    )(strips, pos_row, pos_col, held)

    def whole(*shape):
        return pl.BlockSpec(shape, lambda m: (0,) * len(shape))

    mode_spec = pl.BlockSpec((1, 2, size, size), lambda m: (m, 0, 0, 0))
    table_spec = whole(2 * size, 2 * size)
    buffers = [pltpu.VMEM((2 * size, size), BF16), pltpu.VMEM((size, 2 * size), BF16)]
    far, power = pl.pallas_call(
        forward_kernel,
        grid=(modes,),
        out_shape=(
            jax.ShapeDtypeStruct((modes, 2, size, size), F32),
            jax.ShapeDtypeStruct((size, size), F32),
        ),
        in_specs=[mode_spec, whole(2, size, size), table_spec, table_spec],
        out_specs=(mode_spec, whole(size, size)),
        scratch_shapes=buffers,
        compiler_params=PARAMS,
    )(probe, patch, forward, inverse)
    power = power + swap(power) if groups == 2 else lax.psum(power, "mode")
    term, grad = pl.pallas_call(
        backward_kernel,
        grid=(modes,),
        out_shape=(jax.ShapeDtypeStruct((modes, 2, size, size), BF16), wave_shape),
        in_specs=[
            mode_spec,
            mode_spec,
            whole(2, size, size),
            whole(size, size),
            whole(size, size),
            table_spec,
            table_spec,
        ],
        out_specs=(mode_spec, whole(2, size, size)),
        scratch_shapes=[pltpu.VMEM((size, size), F32)] + buffers,
        compiler_params=PARAMS,
    )(far, probe, patch, amplitude[0], power, inverse, forward)
    probe_grad = lax.psum(term, "scan").astype(F32)

    me = lax.axis_index("mode")
    if groups == 2:
        mine = lax.dynamic_index_in_dim(grad, me, 0, keepdims=True)
        other = lax.dynamic_index_in_dim(grad, 1 - me, 0, keepdims=True)
        grad = mine + swap(other)
    else:
        grad = lax.psum(grad, "mode")
    parts = grad.shape[0]
    pieces = pl.pallas_call(
        place_kernel,
        out_shape=jax.ShapeDtypeStruct((devices, parts, rows, size), F32),
        in_specs=[SMEM, SMEM, VMEM],
        out_specs=VMEM,
        scratch_shapes=[pltpu.VMEM((parts, size + 2 * rows + 8, size), F32)],
        compiler_params=PARAMS,
    )(strips, pos_row, grad)
    received = lax.all_to_all(pieces.astype(BF16), "scan", 0, 0, tiled=False).astype(F32)
    strip_grad = pl.pallas_call(
        add_kernel,
        out_shape=jax.ShapeDtypeStruct((parts, rows, cols), F32),
        in_specs=[SMEM, VMEM],
        out_specs=VMEM,
        scratch_shapes=[pltpu.VMEM((parts, rows, padded_cols), F32)],
        compiler_params=PARAMS,
    )(all_cols, received)
    if groups == 2:
        theirs = swap(strip_grad)
        strip_grad = jnp.where(
            me == 0,
            jnp.concatenate([strip_grad, theirs]),
            jnp.concatenate([theirs, strip_grad]),
        )
    return (strip_grad, probe_grad)


def solution(mesh):
    return jax.shard_map(
        shards,
        mesh=mesh,
        in_specs=(
            P(None, "scan", None),
            P("mode", None, None, None),
            P("scan", None, None),
            P("scan"),
            P("scan"),
            P("scan"),
        ),
        out_specs=(P(None, "scan", None), P("mode", None, None, None)),
        check_vma=False,
    )
```

time: 569 us -> 335 us (0.59); the launches traced: 562 us -> 334 us
  local copies, waits for them, and re-layouts: 109 us -> 1.71 us
  other arithmetic: 87.4 us -> 19.1 us
  waiting for transfers between devices: 266 us -> 203 us
  Pallas kernels: 0 us -> 54.7 us
  matrix products: 31 us -> 0 us
  loops' own time: 29.7 us -> 0 us
  blocking collectives: 16.2 us -> 39.6 us
  starting transfers between devices: 7.2 us -> 0.34 us
    all_to_all x1 -> x0, waiting for transfers between devices: 89.7 us -> none  [shards(): lax.all_to_all(bands, 'scan', split_axis=2, concat_axis=0, tiled=True)]
    all_gather x1, waiting for transfers between devices: 17.7 us -> 74.3 us  [shards(): held = lax.all_gather(packed, 'scan', axis=0)]
    pallas_call x0 -> x5, Pallas kernels: none -> 54.7 us  [the longest x1 22.6 us: shards(): pl.pallas_call(backward_kernel, grid=(modes,), out_shape=(jax.ShapeDtypeS...]
    all_to_all x0 -> x1, blocking collectives: none -> 39.6 us  [shards(): lax.all_to_all(pieces.astype(BF16), 'scan', 0, 0, tiled=False).astype(F32)]
    psum x3 -> x1, waiting for transfers between devices: 159 us -> 121 us  [shards(): probe_grad = lax.psum(term, 'scan').astype(F32)]
    another operation x9 -> x0, other arithmetic: 36 us -> none
    gather x2 -> x0, local copies, waits for them, and re-layouts: 34.4 us -> none  [the longest x1 28.9 us: take_patch(): band_rows = jnp.take(gathered, rows_wanted, axis=1)]
    dot_general x2 -> x0, matrix products: 31 us -> none  [transform(): jnp.einsum('pmiax,oixy->pmoay', half_wave, matrix_table, preferred_elemen...]
  transfers between devices with their start and end apart: 5 -> 5, of which waited for: 5 -> 5; matrix products, arithmetic and copies ran while one was open for 20% -> 2% of each run, Pallas kernels for 0% -> 2%
where the time goes in v1:
time: 335 us; the launch traced here: 334 us
  waiting for transfers between devices  203 us (61%)
  Pallas kernels  54.7 us (16%)
  blocking collectives  39.6 us (12%)
  other arithmetic  19.1 us (6%)
  between operations  16.1 us (5%)
    psum x1, waiting for transfers between devices, shards(): probe_grad = lax.psum(term, 'scan').astype(F32)  121 us
    all_gather x1, waiting for transfers between devices, shards(): held = lax.all_gather(packed, 'scan', axis=0)  74.3 us
    all_to_all x1, blocking collectives, shards(): lax.all_to_all(pieces.astype(BF16), 'scan', 0, 0, tiled=False).astype(F32)  39.6 us
    pallas_call x1, Pallas kernels, shards(): pl.pallas_call(backward_kernel, grid=(modes,), out_shape=(jax.ShapeDtypeS...  22.6 us
    pallas_call x1, Pallas kernels, shards(): pl.pallas_call(forward_kernel, grid=(modes,), out_shape=(jax.ShapeDtypeSt...  19.3 us
    ppermute x3, waiting for transfers between devices, swap(): return lax.ppermute(x, 'mode', [(0, 1), (1, 0)])  7.1 us
    convert_element_type x1, other arithmetic, shards(): probe_grad = lax.psum(term, 'scan').astype(F32)  6.75 us
  transfers between devices with their start and end apart: 5, of which 5 were waited for; matrix products, arithmetic and copies ran while one was open for 2% of the time, Pallas kernels for 2%

profile of v1, /device:TPU:0, one launch (start us, length us, event | category | flops | bytes accessed | tf_op | source)
XLA Modules:
  0.0 334.2 jit_solution(8706299027274362980)
XLA Ops:
  7.2 0.0 all-gather.3.cloned.1.call-start
  8.6 1.0 convert_element_type.24
  9.6 0.7 pad_maximum_fusion
  10.3 0.0 all-gather.3.cloned.1.call-update
  10.3 0.0 all-reduce.2.cloned.1.call-start
  11.0 74.3 %all-gather.3.cloned.1.call-done = bf16[1536,1152]{1,0:T(8,128)(2,1)} async-done(((bf16[96,1152]{1,0:T(8,128)(2,1)}), bf16[1536,1152]{1,0:T(8,128)(2,1)}) %all-gather.3.cloned.1.call-update) | async-done | bytes 3538960 | tf_op jit(solution)/shard_map/all_gather | solution.py:182
  85.3 0.8 slice_convert_fusion
  86.1 0.1 copy.11
  86.2 0.5 slice_bitcast_fusion
  86.7 6.0 %shard_map.95.patch = f32[2,512,512]{2,1,0:T(8,128)} custom-call(s32[16]{0:T(128)} %get-tuple-element.10.strips, s32[1]{0:T(128)S(6)} %copy.13.row, s32[1]{0:T(128)} %copy.14.col, bf16[16,96,1152]{2,1,0:T(8,128)(2,1)} %bitcast.16), custom_call_target="tpu_custom_call" | custom-call | tf_op jit(solution)/shard_map/pallas_call | solution.py:188
  92.7 19.3 %shard_map.96 = (f32[4,2,512,512]{3,2,1,0:T(8,128)}, f32[512,512]{1,0:T(8,128)}) custom-call(f32[4,2,512,512]{3,2,1,0:T(8,128)} %probe.3, f32[2,512,512]{2,1,0:T(8,128)} %shard_map.95.patch, bf16[1024,1024]{1,0:T(8,128)(2,1)} %constant.48.clone.left.right, bf16[1024,1024]{1,0:T(8,128)(2,1)} %constant.49.clone.right.left), custom_call_target="tpu_custom_call" | custom-call | tf_op jit(solution)/shard_map/pallas_call | solution.py:203
  112.0 0.0 collective-permute-start
  112.0 2.9 collective-permute-done
  114.8 2.4 add.29.power
  117.3 22.6 %shard_map.97 = (bf16[4,2,512,512]{3,2,1,0:T(8,128)(2,1)}, f32[2,512,512]{2,1,0:T(8,128)}) custom-call(f32[4,2,512,512]{3,2,1,0:T(8,128)} %get-tuple-element.6.far, f32[4,2,512,512]{3,2,1,0:T(8,128)} %probe.3, f32[2,512,512]{2,1,0:T(8,128)} %shard_map.95.patch, f32[512,512]{1,0:T(8,128)} %bitcast.17, f32[512,512]{1,0:T(8,128)} %add.29.power, ...), custom_call_target="tpu_custom_call" | custom-call | tf_op jit(solution)/shard_map/pallas_call | solution.py:216
  139.8 0.0 copy-start
  139.8 0.0 all-reduce.2.cloned.1.call-update
  139.9 1.6 copy-done
  141.4 0.1 constant_dynamic-slice_fusion
  141.5 0.2 collective-permute-start.1
  141.7 2.7 collective-permute-done.1
  144.4 2.4 dynamic-slice_add_fusion.grad
  146.8 3.0 shard_map.98
  149.8 1.4 convert_element_type.29
  151.2 39.6 %all_to_all.5 = bf16[16,1,40,512]{3,2,1,0:T(8,128)(2,1)S(1)} all-to-all(bf16[16,1,40,512]{3,2,1,0:T(8,128)(2,1)S(1)} %convert_element_type.29), channel_id=1, replica_groups=mesh['scan'=16,'mode'=2] {'scan'}, dimensions={0} | all-to-all | bytes 1310720 | tf_op jit(solution)/shard_map/all_to_all | solution.py:251
  190.8 1.2 convert_element_type.30.received
  192.0 3.9 %shard_map.99 = f32[1,40,1152]{2,1,0:T(8,128)} custom-call(s32[16]{0:T(128)} %get-tuple-element.11.cols, f32[16,1,40,512]{3,2,1,0:T(8,128)} %convert_element_type.30.received), custom_call_target="tpu_custom_call" | custom-call | tf_op jit(solution)/shard_map/pallas_call | solution.py:252
  195.9 0.1 collective-permute-start.2
  196.0 1.6 collective-permute-done.2
  197.6 1.8 maximum_select_fusion
  199.3 121.3 %all-reduce.2.cloned.1.call-done = bf16[4,2,512,512]{3,2,1,0:T(8,128)(2,1)} async-done(((bf16[4,2,512,512]{3,2,1,0:T(8,128)(2,1)}), bf16[4,2,512,512]{3,2,1,0:T(8,128)(2,1)}) %all-reduce.2.cloned.1.call-update) | async-done | bytes 4194320 | tf_op jit(solution)/shard_map/psum | solution.py:233
  320.6 6.7 %convert_element_type.31 = f32[4,2,512,512]{3,2,1,0:T(8,128)} convert(bf16[4,2,512,512]{3,2,1,0:T(8,128)(2,1)} %all-reduce.2.cloned.1.call-done) | non-fusion elementwise | flops 2097152 | bytes 12582912 | tf_op jit(solution)/shard_map/convert_element_type | solution.py:233
  (3 shorter events, 0.0 us)
Async XLA Ops:
  7.2 78.2 %all-gather.3.cloned.1.call-start = ((), (), s32[]{:S(2)}) async-start(), calls=%async_computation.2 | async-start | bytes 3760128 | tf_op jit(solution)/shard_map/all_gather | solution.py:182
  10.3 310.3 %all-reduce.2.cloned.1.call-start = ((), (), s32[]{:S(2)}) async-start(), calls=%async_computation.1 | async-start | bytes 8388608 | tf_op jit(solution)/shard_map/psum | solution.py:233
  112.0 2.9 collective-permute-start
  139.8 1.6 copy-start
  141.5 2.9 collective-permute-start.1
  195.9 1.6 collective-permute-start.2
Sparse Core Ops, SparseCore 0:
  11.4 73.9 all-gather.2
  140.0 180.5 all-reduce.1

commit v2 on v1

--- a/solution.py
+++ b/solution.py
@@ -11,7 +11,8 @@
 F32 = jnp.float32
 BF16 = jnp.bfloat16
 LANES = 128
-META = 16
+META = 8
+PLANE = 4
 TILE = 256
 PARAMS = pltpu.CompilerParams(vmem_limit_bytes=56 * 1024 * 1024)
 VMEM = pl.BlockSpec(memory_space=pltpu.VMEM)
@@ -29,16 +30,64 @@
     return jnp.asarray(forward, BF16), jnp.asarray(inverse, BF16)
 
 
+def gather_kernel(mine, out, line_send, line_recv, plane_send, plane_recv, swap_send, swap_recv):
+    count = out.shape[1]
+    lines = count // PLANE
+    scan, mode = lax.axis_index("scan"), lax.axis_index("mode")
+    line, place = scan // PLANE, lax.rem(scan, PLANE)
+    in_line = [(lax.rem(line + k, lines) * PLANE + place, mode) for k in range(1, lines)]
+    in_plane = [(line * PLANE + lax.rem(place + t, PLANE), mode) for t in range(1, PLANE)]
+    partner = (scan, 1 - mode)
+
+    barrier = pltpu.get_barrier_semaphore()
+    for peer in in_line + in_plane + [partner]:
+        pl.semaphore_signal(barrier, inc=1, device_id=peer, device_id_type=pl.DeviceIdType.MESH)
+    pl.semaphore_wait(barrier, len(in_line) + len(in_plane) + 1)
+
+    def push(src, dst, send, recv, peer):
+        copy = pltpu.make_async_remote_copy(
+            src_ref=src,
+            dst_ref=dst,
+            send_sem=send,
+            recv_sem=recv,
+            device_id=peer,
+            device_id_type=pl.DeviceIdType.MESH,
+        )
+        copy.start()
+        return copy
+
+    own = out.at[mode, scan]
+    line_copies = [
+        push(mine, own, line_send.at[k], line_recv.at[k], peer) for k, peer in enumerate(in_line)
+    ]
+    plane_copies = [
+        push(mine, own, plane_send.at[0, t], plane_recv.at[0, t], peer) for t, peer in enumerate(in_plane)
+    ]
+    out[mode, scan] = mine[...]
+    for k, arriving in enumerate(line_copies):
+        arriving.wait_recv()
+        piece = out.at[mode, lax.rem(line + lines - k - 1, lines) * PLANE + place]
+        plane_copies += [
+            push(piece, piece, plane_send.at[k + 1, t], plane_recv.at[k + 1, t], peer)
+            for t, peer in enumerate(in_plane)
+        ]
+    for copy in plane_copies:
+        copy.wait_recv()
+    last = push(out.at[mode], out.at[mode], swap_send, swap_recv, partner)
+    for copy in line_copies + plane_copies:
+        copy.wait_send()
+    last.wait()
+
+
 def cut_kernel(strips, row, col, held, patch, window):
-    count, rows = held.shape[0], (held.shape[1] - META) // 2
+    count, rows = held.shape[1], held.shape[2] - META
     size, cols = patch.shape[-1], held.shape[-1]
     wide = size + LANES
 
     def place(j, carry):
-        both = held[j][: 2 * rows].astype(F32)
         at = pl.ds(pl.multiple_of(strips[j] * rows, 8), rows)
-        window[0, at, :cols] = both[:rows]
-        window[1, at, :cols] = both[rows:]
+        for c in range(2):
+            window[c, at, :cols] = held[c, j].astype(F32)[:rows]
         return carry
 
     lax.fori_loop(0, count, place, 0)
@@ -176,11 +225,32 @@
     def swap(x):
         return lax.ppermute(x, "mode", [(0, 1), (1, 0)])
 
-    lane = lax.broadcasted_iota(jnp.int32, (META, cols), 1)
+    lane = lax.broadcasted_iota(jnp.int32, (2, META, cols), 2)
     numbers = jnp.where(lane == 0, strip_of[0], jnp.where(lane == 1, pos_col[0] // LANES, pos_col[0] % LANES))
-    packed = jnp.concatenate([object_field.reshape(2 * rows, cols).astype(BF16), numbers.astype(BF16)])
-    held = lax.all_gather(packed, "scan", axis=0)
-    numbers = held[:, 2 * rows, :3].astype(jnp.int32)
+    packed = jnp.concatenate([object_field.astype(BF16), numbers.astype(BF16)], axis=1)
+    me = lax.axis_index("mode")
+    if groups == 2 and devices % PLANE == 0:
+        dma, lines = pltpu.SemaphoreType.DMA, devices // PLANE
+        held = pl.pallas_call(
+            gather_kernel,
+            out_shape=jax.ShapeDtypeStruct((2, devices, rows + META, cols), BF16),
+            in_specs=[VMEM],
+            out_specs=VMEM,
+            scratch_shapes=[
+                dma((max(lines - 1, 1),)),
+                dma((max(lines - 1, 1),)),
+                dma((lines, PLANE - 1)),
+                dma((lines, PLANE - 1)),
+                dma,
+                dma,
+            ],
+            compiler_params=pltpu.CompilerParams(
+                vmem_limit_bytes=56 * 1024 * 1024, collective_id=0, has_side_effects=True
+            ),
+        )(lax.dynamic_index_in_dim(packed, me, 0, keepdims=False))
+    else:
+        held = lax.all_gather(packed, "scan", axis=1)
+    numbers = held[0, :, rows, :3].astype(jnp.int32)
     strips = numbers[:, 0]
     all_cols = numbers[:, 1] * LANES + numbers[:, 2]
 
@@ -232,7 +302,6 @@
     )(far, probe, patch, amplitude[0], power, inverse, forward)
     probe_grad = lax.psum(term, "scan").astype(F32)
 
-    me = lax.axis_index("mode")
     if groups == 2:
         mine = lax.dynamic_index_in_dim(grad, me, 0, keepdims=True)
         other = lax.dynamic_index_in_dim(grad, 1 - me, 0, keepdims=True)

time: 335 us -> 294 us (0.88)
  waiting for transfers between devices: 203 us -> 128 us
  Pallas kernels: 54.7 us -> 87 us
    all_gather x1 -> x0, waiting for transfers between devices: 74.3 us -> none  [shards(): held = lax.all_gather(packed, 'scan', axis=0)]
    pallas_call x0 -> x1, Pallas kernels: none -> 32.3 us  [shards(): pl.pallas_call(gather_kernel, out_shape=jax.ShapeDtypeStruct((2, devices,...]
  transfers between devices with their start and end apart: 5 -> 4, of which waited for: 5 -> 4; matrix products, arithmetic and copies ran while one was open for 2% -> 2% of each run, Pallas kernels for 2% -> 2%
where the time goes in v2:
time: 294 us; the launch traced here: 293 us
  waiting for transfers between devices  128 us (44%)
  Pallas kernels  87 us (30%)
  blocking collectives  41.3 us (14%)
  other arithmetic  17.9 us (6%)
  between operations  16.1 us (5%)
    psum x1, waiting for transfers between devices, shards(): probe_grad = lax.psum(term, 'scan').astype(F32)  122 us
    all_to_all x1, blocking collectives, shards(): lax.all_to_all(pieces.astype(BF16), 'scan', 0, 0, tiled=False).astype(F32)  41.3 us
    pallas_call x1, Pallas kernels, shards(): pl.pallas_call(gather_kernel, out_shape=jax.ShapeDtypeStruct((2, devices,...  32.3 us
    pallas_call x1, Pallas kernels, shards(): pl.pallas_call(backward_kernel, grid=(modes,), out_shape=(jax.ShapeDtypeS...  22.6 us
    pallas_call x1, Pallas kernels, shards(): pl.pallas_call(forward_kernel, grid=(modes,), out_shape=(jax.ShapeDtypeSt...  19.2 us
    convert_element_type x1, other arithmetic, shards(): probe_grad = lax.psum(term, 'scan').astype(F32)  6.75 us
    ppermute x3, waiting for transfers between devices, swap(): return lax.ppermute(x, 'mode', [(0, 1), (1, 0)])  6.42 us
    pallas_call x1, Pallas kernels, shards(): pl.pallas_call(cut_kernel, out_shape=wave_shape, in_specs=[SMEM, SMEM, SM...  6 us
  transfers between devices with their start and end apart: 4, of which 4 were waited for; matrix products, arithmetic and copies ran while one was open for 2% of the time, Pallas kernels for 2%

profile of v2, /device:TPU:0, one launch (start us, length us, event | category | flops | bytes accessed | tf_op | source)
XLA Modules:
  0.0 293.1 jit_solution(4892865350425346519)
XLA Ops:
  7.2 0.0 all-reduce.2.cloned.1.call-start
  7.9 1.0 convert_element_type.21
  9.6 0.7 fusion.1.mine
  10.3 32.3 %shard_map.95.held = bf16[2,16,48,1152]{3,2,1,0:T(8,128)(2,1)} custom-call(bf16[48,1152]{1,0:T(8,128)(2,1)} %fusion.1.mine), custom_call_target="tpu_custom_call" | custom-call | tf_op jit(solution)/shard_map/pallas_call | solution.py:234
  42.6 0.8 slice_convert_fusion
  43.3 0.1 copy.11
  43.4 0.6 slice_bitcast_fusion
  44.7 6.0 %shard_map.96.patch = f32[2,512,512]{2,1,0:T(8,128)} custom-call(s32[16]{0:T(128)} %get-tuple-element.10.strips, s32[1]{0:T(128)S(6)} %copy.13.row, s32[1]{0:T(128)} %copy.14.col, bf16[2,16,48,1152]{3,2,1,0:T(8,128)(2,1)} %shard_map.95.held), custom_call_target="tpu_custom_call" | custom-call | tf_op jit(solution)/shard_map/pallas_call | solution.py:258
  50.7 19.2 %shard_map.97 = (f32[4,2,512,512]{3,2,1,0:T(8,128)}, f32[512,512]{1,0:T(8,128)}) custom-call(f32[4,2,512,512]{3,2,1,0:T(8,128)} %probe.3, f32[2,512,512]{2,1,0:T(8,128)} %shard_map.96.patch, bf16[1024,1024]{1,0:T(8,128)(2,1)} %constant.52.clone.left.right, bf16[1024,1024]{1,0:T(8,128)(2,1)} %constant.53.clone.right.left), custom_call_target="tpu_custom_call" | custom-call | tf_op jit(solution)/shard_map/pallas_call | solution.py:273
  69.9 0.4 collective-permute-start
  70.3 2.5 collective-permute-done
  72.8 2.4 add.32.power
  75.2 22.6 %shard_map.98 = (bf16[4,2,512,512]{3,2,1,0:T(8,128)(2,1)}, f32[2,512,512]{2,1,0:T(8,128)}) custom-call(f32[4,2,512,512]{3,2,1,0:T(8,128)} %get-tuple-element.6.far, f32[4,2,512,512]{3,2,1,0:T(8,128)} %probe.3, f32[2,512,512]{2,1,0:T(8,128)} %shard_map.96.patch, f32[512,512]{1,0:T(8,128)} %bitcast.15, f32[512,512]{1,0:T(8,128)} %add.32.power, ...), custom_call_target="tpu_custom_call" | custom-call | tf_op jit(solution)/shard_map/pallas_call | solution.py:286
  97.8 0.0 copy-start
  97.8 0.0 all-reduce.2.cloned.1.call-update
  97.8 1.6 copy-done
  99.4 0.1 constant_dynamic-slice_fusion
  99.5 0.4 collective-permute-start.1
  99.9 2.3 collective-permute-done.1
  102.2 1.3 dynamic-slice_add_fusion.grad
  103.4 3.1 %shard_map.99 = f32[16,1,40,512]{3,2,1,0:T(8,128)} custom-call(s32[16]{0:T(128)} %get-tuple-element.10.strips, s32[1]{0:T(128)S(6)} %copy.13.row, f32[1,512,512]{2,1,0:T(8,128)} %dynamic-slice_add_fusion.grad), custom_call_target="tpu_custom_call" | custom-call | tf_op jit(solution)/shard_map/pallas_call | solution.py:312
  106.5 1.4 convert_element_type.25
  107.9 41.3 %all_to_all.5 = bf16[16,1,40,512]{3,2,1,0:T(8,128)(2,1)S(1)} all-to-all(bf16[16,1,40,512]{3,2,1,0:T(8,128)(2,1)S(1)} %convert_element_type.25), channel_id=1, replica_groups=mesh['scan'=16,'mode'=2] {'scan'}, dimensions={0} | all-to-all | bytes 1310720 | tf_op jit(solution)/shard_map/all_to_all | solution.py:320
  149.2 1.2 convert_element_type.26.received
  150.5 3.9 %shard_map.100 = f32[1,40,1152]{2,1,0:T(8,128)} custom-call(s32[16]{0:T(128)} %get-tuple-element.11.cols, f32[16,1,40,512]{3,2,1,0:T(8,128)} %convert_element_type.26.received), custom_call_target="tpu_custom_call" | custom-call | tf_op jit(solution)/shard_map/pallas_call | solution.py:321
  154.3 0.0 collective-permute-start.2
  154.3 1.6 collective-permute-done.2
  156.0 1.8 maximum_select_fusion
  157.7 121.8 %all-reduce.2.cloned.1.call-done = bf16[4,2,512,512]{3,2,1,0:T(8,128)(2,1)} async-done(((bf16[4,2,512,512]{3,2,1,0:T(8,128)(2,1)}), bf16[4,2,512,512]{3,2,1,0:T(8,128)(2,1)}) %all-reduce.2.cloned.1.call-update) | async-done | bytes 4194320 | tf_op jit(solution)/shard_map/psum | solution.py:303
  279.5 6.7 %convert_element_type.27 = f32[4,2,512,512]{3,2,1,0:T(8,128)} convert(bf16[4,2,512,512]{3,2,1,0:T(8,128)(2,1)} %all-reduce.2.cloned.1.call-done) | non-fusion elementwise | flops 2097152 | bytes 12582912 | tf_op jit(solution)/shard_map/convert_element_type | solution.py:303
  (3 shorter events, 0.0 us)
Async XLA Ops:
  7.2 272.3 %all-reduce.2.cloned.1.call-start = ((), (), s32[]{:S(2)}) async-start(), calls=%async_computation.1 | async-start | bytes 8388608 | tf_op jit(solution)/shard_map/psum | solution.py:303
  69.9 2.9 collective-permute-start
  97.8 1.6 copy-start
  99.5 2.7 collective-permute-start.1
  154.3 1.6 collective-permute-start.2
Sparse Core Ops, SparseCore 0:
  97.9 181.5 all-reduce.1

commit v3 on v2

--- a/solution.py
+++ b/solution.py
@@ -283,24 +283,30 @@
         compiler_params=PARAMS,
     )(probe, patch, forward, inverse)
     power = power + swap(power) if groups == 2 else lax.psum(power, "mode")
-    term, grad = pl.pallas_call(
-        backward_kernel,
-        grid=(modes,),
-        out_shape=(jax.ShapeDtypeStruct((modes, 2, size, size), BF16), wave_shape),
-        in_specs=[
-            mode_spec,
-            mode_spec,
-            whole(2, size, size),
-            whole(size, size),
-            whole(size, size),
-            table_spec,
-            table_spec,
-        ],
-        out_specs=(mode_spec, whole(2, size, size)),
-        scratch_shapes=[pltpu.VMEM((size, size), F32)] + buffers,
-        compiler_params=PARAMS,
-    )(far, probe, patch, amplitude[0], power, inverse, forward)
-    probe_grad = lax.psum(term, "scan").astype(F32)
+    cuts = [0, modes // 2, modes] if modes > 1 else [0, modes]
+    probe_parts, grad = [], 0.0
+    for low, high in zip(cuts[:-1], cuts[1:]):
+        from_spec = pl.BlockSpec((1, 2, size, size), lambda m, low=low: (m + low, 0, 0, 0))
+        term, grad_part = pl.pallas_call(
+            backward_kernel,
+            grid=(high - low,),
+            out_shape=(jax.ShapeDtypeStruct((high - low, 2, size, size), BF16), wave_shape),
+            in_specs=[
+                from_spec,
+                from_spec,
+                whole(2, size, size),
+                whole(size, size),
+                whole(size, size),
+                table_spec,
+                table_spec,
+            ],
+            out_specs=(mode_spec, whole(2, size, size)),
+            scratch_shapes=[pltpu.VMEM((size, size), F32)] + buffers,
+            compiler_params=PARAMS,
+        )(far, probe, patch, amplitude[0], power, inverse, forward)
+        probe_parts.append(lax.psum(term, "scan"))
+        grad = grad + grad_part
+    probe_grad = jnp.concatenate(probe_parts).astype(F32)
 
     if groups == 2:
         mine = lax.dynamic_index_in_dim(grad, me, 0, keepdims=True)

time: 294 us -> 300 us (1.020)
  Pallas kernels: 87 us -> 93.7 us
    pallas_call x1 -> x2, Pallas kernels: 22.6 us -> 29.2 us  [shards(): pl.pallas_call(backward_kernel, grid=(high - low,), out_shape=(jax.ShapeD...]
  transfers between devices with their start and end apart: 4 -> 4, of which waited for: 4 -> 4; matrix products, arithmetic and copies ran while one was open for 2% -> 3% of each run, Pallas kernels for 2% -> 2%
where the time goes in v3:
time: 300 us
  waiting for transfers between devices  128 us (43%)
  Pallas kernels  93.7 us (31%)
  blocking collectives  39.9 us (13%)
  other arithmetic  19.3 us (6%)
  between operations  16.1 us (5%)
    psum x1, waiting for transfers between devices, shards(): probe_parts.append(lax.psum(term, 'scan'))  122 us
    all_to_all x1, blocking collectives, shards(): lax.all_to_all(pieces.astype(BF16), 'scan', 0, 0, tiled=False).astype(F32)  39.9 us
    pallas_call x1, Pallas kernels, shards(): pl.pallas_call(gather_kernel, out_shape=jax.ShapeDtypeStruct((2, devices,...  32.3 us
    pallas_call x2, Pallas kernels, shards(): pl.pallas_call(backward_kernel, grid=(high - low,), out_shape=(jax.ShapeD...  29.2 us
    pallas_call x1, Pallas kernels, shards(): pl.pallas_call(forward_kernel, grid=(modes,), out_shape=(jax.ShapeDtypeSt...  19.3 us
    ppermute x3, waiting for transfers between devices, swap(): return lax.ppermute(x, 'mode', [(0, 1), (1, 0)])  6.29 us
    convert_element_type x1, other arithmetic, shards(): probe_grad = jnp.concatenate(probe_parts).astype(F32)  6.16 us
    pallas_call x1, Pallas kernels, shards(): pl.pallas_call(cut_kernel, out_shape=wave_shape, in_specs=[SMEM, SMEM, SM...  6.01 us
  transfers between devices with their start and end apart: 4, of which 4 were waited for; matrix products, arithmetic and copies ran while one was open for 3% of the time, Pallas kernels for 2%

profile of v3, /device:TPU:0, one launch (start us, length us, event | category | flops | bytes accessed | tf_op | source)
XLA Modules:
  0.0 299.7 jit_solution(11539359890325585853)
XLA Ops:
  7.2 0.0 all-reduce.3.cloned.1.call-start
  7.9 1.0 convert_element_type.21
  9.6 0.7 fusion.1.mine
  10.3 32.3 %shard_map.95.held = bf16[2,16,48,1152]{3,2,1,0:T(8,128)(2,1)} custom-call(bf16[48,1152]{1,0:T(8,128)(2,1)} %fusion.1.mine), custom_call_target="tpu_custom_call" | custom-call | tf_op jit(solution)/shard_map/pallas_call | solution.py:234
  42.6 0.8 slice_convert_fusion
  43.3 0.1 copy.11
  43.4 0.5 slice_bitcast_fusion
  44.6 6.0 %shard_map.96.patch = f32[2,512,512]{2,1,0:T(8,128)} custom-call(s32[16]{0:T(128)} %get-tuple-element.16.strips, s32[1]{0:T(128)S(6)} %copy.14.row, s32[1]{0:T(128)} %copy.15.col, bf16[2,16,48,1152]{3,2,1,0:T(8,128)(2,1)} %shard_map.95.held), custom_call_target="tpu_custom_call" | custom-call | tf_op jit(solution)/shard_map/pallas_call | solution.py:258
  50.6 19.3 %shard_map.97 = (f32[4,2,512,512]{3,2,1,0:T(8,128)}, f32[512,512]{1,0:T(8,128)}) custom-call(f32[4,2,512,512]{3,2,1,0:T(8,128)} %probe.5, f32[2,512,512]{2,1,0:T(8,128)} %shard_map.96.patch, bf16[1024,1024]{1,0:T(8,128)(2,1)} %constant.52.clone.left.right, bf16[1024,1024]{1,0:T(8,128)(2,1)} %constant.53.clone.right.left), custom_call_target="tpu_custom_call" | custom-call | tf_op jit(solution)/shard_map/pallas_call | solution.py:273
  69.9 0.4 collective-permute-start
  70.2 2.5 collective-permute-done
  72.7 2.4 add.37.power
  75.2 14.6 %shard_map.98 = (bf16[2,2,512,512]{3,2,1,0:T(8,128)(2,1)}, f32[2,512,512]{2,1,0:T(8,128)}) custom-call(f32[4,2,512,512]{3,2,1,0:T(8,128)} %get-tuple-element.8.far, f32[4,2,512,512]{3,2,1,0:T(8,128)} %probe.5, f32[2,512,512]{2,1,0:T(8,128)} %shard_map.96.patch, f32[512,512]{1,0:T(8,128)} %bitcast.15, f32[512,512]{1,0:T(8,128)} %add.37.power, ...), custom_call_target="tpu_custom_call" | custom-call | tf_op jit(solution)/shard_map/pallas_call | solution.py:290
  89.8 14.6 %shard_map.99 = (bf16[2,2,512,512]{3,2,1,0:T(8,128)(2,1)}, f32[2,512,512]{2,1,0:T(8,128)}) custom-call(f32[4,2,512,512]{3,2,1,0:T(8,128)} %get-tuple-element.8.far, f32[4,2,512,512]{3,2,1,0:T(8,128)} %probe.5, f32[2,512,512]{2,1,0:T(8,128)} %shard_map.96.patch, f32[512,512]{1,0:T(8,128)} %bitcast.16, f32[512,512]{1,0:T(8,128)} %add.37.power, ...), custom_call_target="tpu_custom_call" | custom-call | tf_op jit(solution)/shard_map/pallas_call | solution.py:290
  104.4 0.0 copy-start
  104.4 0.0 all-reduce.3.cloned.1.call-update
  104.4 1.6 copy-done
  106.0 2.1 add.38
  108.0 0.1 constant_dynamic-slice_fusion
  108.1 0.4 collective-permute-start.1
  108.6 2.3 collective-permute-done.1
  110.8 1.3 dynamic-slice_add_fusion.grad
  112.1 3.0 %shard_map.100 = f32[16,1,40,512]{3,2,1,0:T(8,128)} custom-call(s32[16]{0:T(128)} %get-tuple-element.16.strips, s32[1]{0:T(128)S(6)} %copy.14.row, f32[1,512,512]{2,1,0:T(8,128)} %dynamic-slice_add_fusion.grad), custom_call_target="tpu_custom_call" | custom-call | tf_op jit(solution)/shard_map/pallas_call | solution.py:318
  115.1 1.4 convert_element_type.25
  116.5 39.9 %all_to_all.5 = bf16[16,1,40,512]{3,2,1,0:T(8,128)(2,1)S(1)} all-to-all(bf16[16,1,40,512]{3,2,1,0:T(8,128)(2,1)S(1)} %convert_element_type.25), channel_id=1, replica_groups=mesh['scan'=16,'mode'=2] {'scan'}, dimensions={0} | all-to-all | bytes 1310720 | tf_op jit(solution)/shard_map/all_to_all | solution.py:326
  156.5 1.2 convert_element_type.26.received
  157.7 3.9 %shard_map.101 = f32[1,40,1152]{2,1,0:T(8,128)} custom-call(s32[16]{0:T(128)} %get-tuple-element.17.cols, f32[16,1,40,512]{3,2,1,0:T(8,128)} %convert_element_type.26.received), custom_call_target="tpu_custom_call" | custom-call | tf_op jit(solution)/shard_map/pallas_call | solution.py:327
  161.6 0.1 collective-permute-start.2
  161.7 1.5 collective-permute-done.2
  163.2 1.8 maximum_select_fusion
  165.0 121.7 %all-reduce.3.cloned.1.call-done = (bf16[2,2,512,512]{3,2,1,0:T(8,128)(2,1)}, bf16[2,2,512,512]{3,2,1,0:T(8,128)(2,1)}) async-done(((bf16[2,2,512,512]{3,2,1,0:T(8,128)(2,1)}, bf16[2,2,512,512]{3,2,1,0:T(8,128)(2,1)}), (bf16[2,2,512,512]{3,2,1,0:T(8,128)(2,1)}, bf16[2,2,512,512]{3,2,1,0:T(8,128)(2,1)})) %all-reduce.3.cloned.1.call-update) | async-done | bytes 4194320 | tf_op jit(solution)/shard_map/psum | solution.py:307
  286.7 6.2 %maximum_convert_fusion = f32[4,2,512,512]{3,2,1,0:T(8,128)} fusion(bf16[2,2,512,512]{3,2,1,0:T(8,128)(2,1)} %get-tuple-element.14, bf16[2,2,512,512]{3,2,1,0:T(8,128)(2,1)} %get-tuple-element.15), kind=kLoop, calls=%fused_computation | loop fusion | flops 4194304 | bytes 12582912 | tf_op jit(solution)/shard_map/convert_element_type | solution.py:309
  (3 shorter events, 0.0 us)
Async XLA Ops:
  7.2 279.5 %all-reduce.3.cloned.1.call-start = ((), (), s32[]{:S(2)}) async-start(), calls=%async_computation.1 | async-start | bytes 8388608 | tf_op jit(solution)/shard_map/psum | solution.py:307
  69.9 2.9 collective-permute-start
  104.4 1.6 copy-start
  108.1 2.7 collective-permute-start.1
  161.6 1.6 collective-permute-start.2
Sparse Core Ops, SparseCore 0:
  104.5 182.1 all-reduce.2
